TPU v7x, 32 devices: a whole 2x2x4 slice. The times are simulated.
32 devices in a mesh: group: 2 (over y), dp: 16 (over z, x, core).
Axes of the slice: x: 2, y: 2, z: 4, core: 2. Of those that a mesh axis runs over, the one named last changes fastest.
Arguments:
- clips_feat: bfloat16 [4096, 4096], P(('group', 'dp')), parts along dimension 0, may hold values from -6 to 6
- weight: bfloat16 [4096, 384], P('dp'), may hold values from -0.09375 to 0.09375
- sentences: bfloat16 [4096, 384], P(('group', 'dp')), parts along dimension 0, may hold values from -6 to 6
- log_scale: float32 [1], replicated, may hold values from 4.3 to 4.6
- bias: float32 [1], replicated, may hold values from -14 to -11
- positives: int32 [4096, 2], P(('group', 'dp')), parts along dimension 0, may hold values from 0 to 2047
Outputs:
- clip_loss: float32 [4096], P(('group', 'dp')), parts along dimension 0
- grad_weight: float32 [8192, 384], P(('group', 'dp')), parts along dimension 0
- grad_scalars: float32 [4], P('group'), parts along dimension 0
There are 2 independent parts, one for each index of `group`. A program takes and returns all parts, laid end to end along the dimension named above; an argument that names none is the same for every part. Nothing has to cross between parts.
Inputs may be any that keep to these rules, and one draw needn't show every extreme that they name: `positives`: two sentence ids for each clip; they may coincide.
All inputs are finite; a program needn't handle non-finite values.
Results may differ from a plain program's by a relative error of at most 0.002.
The roundings to bfloat16 on the way count: a program that leaves them out, or rounds other values in their place, can miss the bound.
Values may be sent and summed in bfloat16 or wider, within the bound.
A program may use at most 64 MiB of HBM per device.

v0:
```python
import jax
import jax.numpy as jnp
from jax import lax
from jax.sharding import PartitionSpec as P

column_block = 2048


def swapped(x, axis, apart):
    return lax.ppermute(x, axis, [(i, i ^ 1 << apart) for i in range(lax.axis_size(axis))])


def shards(clips_feat, weight, sentences, log_scale, bias, positives):
    rows_here = clips_feat.shape[0]
    embed_width = weight.shape[1]
    devices = lax.axis_size("dp")
    position = lax.axis_index("dp")
    full_weight = lax.all_gather(weight, "dp", axis=0, tiled=True)
    proj = jnp.dot(clips_feat, full_weight, preferred_element_type=jnp.float32)
    inverse = lax.rsqrt(jnp.sum(proj * proj, axis=1, keepdims=True) + 1e-06)
    unit32 = proj * inverse
    clip_unit = unit32.astype(jnp.bfloat16)
    sent32 = sentences.astype(jnp.float32)
    sent_unit = (
        sent32 * lax.rsqrt(jnp.sum(sent32 * sent32, axis=1, keepdims=True) + 1e-06)
    ).astype(jnp.bfloat16)
    scale = jnp.exp(log_scale[0])
    shift = bias[0]
    inv_count = 1.0 / (rows_here * devices)
    first_pos = positives[:, 0:1]
    second_pos = positives[:, 1:2]

    def one_tile(carry, block, start):
        losses, grad, dscale, dbias = carry
        span = block.shape[0]
        products = lax.dot_general(
            clip_unit, block, (((1,), (1,)), ((), ())), preferred_element_type=jnp.float32
        )
        logits = scale * products + shift
        columns = start + lax.iota(jnp.int32, span)
        matched = (first_pos == columns[None, :]) | (second_pos == columns[None, :])
        target = jnp.where(matched, jnp.float32(1.0), jnp.float32(-1.0))
        margin = target * logits
        losses = losses - jnp.sum(jax.nn.log_sigmoid(margin), axis=1)
        grad_logit = -target * jax.nn.sigmoid(-margin) * inv_count
        dscale = dscale + jnp.sum(grad_logit * (scale * products))
        dbias = dbias + jnp.sum(grad_logit)
        grad = grad + jnp.dot(
            grad_logit.astype(jnp.bfloat16), block, preferred_element_type=jnp.float32
        )
        return (losses, grad, dscale, dbias)

    def tile_rows(carry, piece, start):
        span = piece.shape[0]
        if span > column_block and span % column_block == 0:
            stacked = piece.reshape(span // column_block, column_block, embed_width)
            offsets = start + column_block * lax.iota(jnp.int32, span // column_block)

            def step_once(inner_carry, inputs):
                return (one_tile(inner_carry, inputs[0], inputs[1]), None)

            result, unused = lax.scan(step_once, carry, (stacked, offsets))
            return result
        return one_tile(carry, piece, start)

    initial = (
        jnp.zeros((rows_here,), jnp.float32),
        jnp.zeros((rows_here, embed_width), jnp.float32),
        jnp.float32(0.0),
        jnp.float32(0.0),
    )
    carry = tile_rows(initial, sent_unit, position * rows_here)
    buffer = sent_unit
    levels = devices.bit_length() - 1
    for level in range(levels):
        other = swapped(buffer, "dp", level)
        stride = 1 << level
        partner_base = jnp.bitwise_xor(position, stride) // stride * stride
        carry = tile_rows(carry, other, partner_base * rows_here)
        if level + 1 < levels:
            upper = position // stride % 2 == 1
            buffer = jnp.where(
                upper,
                jnp.concatenate([other, buffer], axis=0),
                jnp.concatenate([buffer, other], axis=0),
            )
    clip_loss, grad, dscale, dbias = carry
    grad_unit = scale * grad
    inner = jnp.sum(unit32 * grad_unit, axis=1, keepdims=True)
    grad_proj = (inverse * (grad_unit - unit32 * inner)).astype(jnp.bfloat16)
    grad_weight = lax.psum_scatter(
        lax.dot_general(
            clips_feat, grad_proj, (((0,), (0,)), ((), ())), preferred_element_type=jnp.float32
        ),
        "dp",
        scatter_dimension=0,
        tiled=True,
    )
    summed = lax.psum((dscale, dbias), "dp")
    grad_scalars = jnp.stack([summed[0], summed[1]])
    return (clip_loss, grad_weight, grad_scalars)


def solution(mesh):
    in_specs = (
        P(("group", "dp"), None),
        P("dp", None),
        P(("group", "dp"), None),
        P(),
        P(),
        P(("group", "dp"), None),
    )
    out_specs = (P(("group", "dp")), P(("group", "dp"), None), P("group"))
    return jax.shard_map(shards, mesh=mesh, in_specs=in_specs, out_specs=out_specs, check_vma=False)
```

profile of v0, /device:TPU:0, one launch (start us, length us, event | category | flops | bytes accessed | tf_op | source)
XLA Modules:
  0.0 191.8 jit_solution(283245672790788973)
XLA Ops:
  7.2 0.0 copy-start
  7.2 0.0 all-gather.2.cloned.1.call-start
  7.2 0.7 all-gather.2.cloned.1.call-update
  7.9 0.0 reduce-scatter.2.cloned.1.call-start
  8.0 1.0 fusion.12
  9.0 1.0 fusion.13
  10.0 0.5 collective-permute-start
  11.8 0.0 collective-permute-done
  11.9 2.7 %collective-permute-start.1 = (bf16[256,384]{1,0:T(8,128)(2,1)S(1)}, bf16[256,384]{1,0:T(8,128)(2,1)S(1)}, u32[]{:S(2)}, u32[]{:S(2)}) collective-permute-start(bf16[256,384]{1,0:T(8,128)(2,1)S(1)} %maximum_select_fusion.2), channel_id=1, source_target_pairs={{0,2},{1,3},{2,0},{3,1},{4,6},{5,7},{6,4},{7,5},{8,10},{9,11},{10,... | collective-permute-start | bytes 589832 | tf_op jit(solution)/shard_map/ppermute | solution.py:10
  14.6 5.4 %collective-permute-done.1 = bf16[256,384]{1,0:T(8,128)(2,1)S(1)} collective-permute-done((bf16[256,384]{1,0:T(8,128)(2,1)S(1)}, bf16[256,384]{1,0:T(8,128)(2,1)S(1)}, u32[]{:S(2)}, u32[]{:S(2)}) %collective-permute-start.1) | collective-permute-done | bytes 196640 | tf_op jit(solution)/shard_map/ppermute | solution.py:10
  20.0 0.1 maximum_select_fusion.1
  20.2 1.9 collective-permute-start.2
  22.1 0.8 slice_bitcast_fusion.1
  22.8 14.6 %collective-permute-done.2 = bf16[512,384]{1,0:T(8,128)(2,1)S(1)} collective-permute-done((bf16[512,384]{1,0:T(8,128)(2,1)S(1)}, bf16[512,384]{1,0:T(8,128)(2,1)S(1)}, u32[]{:S(2)}, u32[]{:S(2)}) %collective-permute-start.2) | collective-permute-done | bytes 393248 | tf_op jit(solution)/shard_map/ppermute | solution.py:10
  37.4 0.3 maximum_select_fusion
  37.7 2.7 %collective-permute-start.3 = (bf16[1024,384]{1,0:T(8,128)(2,1)S(1)}, bf16[1024,384]{1,0:T(8,128)(2,1)S(1)}, u32[]{:S(2)}, u32[]{:S(2)}) collective-permute-start(bf16[1024,384]{1,0:T(8,128)(2,1)S(1)} %maximum_select_fusion), channel_id=1, source_target_pairs={{0,8},{1,9},{2,10},{3,11},{4,12},{5,13},{6,14},{7,15},{8,0},{9,1},... | collective-permute-start | bytes 2359304 | tf_op jit(solution)/shard_map/ppermute | solution.py:10
  40.4 39.4 %all-gather.2.cloned.1.call-done = bf16[4096,384]{1,0:T(8,128)(2,1)} async-done(((bf16[256,384]{1,0:T(8,128)(2,1)}), bf16[4096,384]{1,0:T(8,128)(2,1)}) %all-gather.2.cloned.1.call-update) | async-done | bytes 3145744 | tf_op jit(solution)/shard_map/all_gather | solution.py:18
  79.8 0.0 copy-done
  79.8 2.7 %multiply_reduce_fusion.3 = (f32[128]{0:T(128)S(1)}, f32[128,384]{1,0:T(8,128)S(1)}) fusion(bf16[128,4096]{1,0:T(8,128)(2,1)S(1)} %copy-done, bf16[4096,384]{1,0:T(8,128)(2,1)} %all-gather.2.cloned.1.call-done), kind=kOutput, calls=%fused_computation.39 | convolution fusion | flops 402751360 | bytes 4391424 | tf_op jit(solution)/shard_map/dot_general | solution.py:19
  82.5 0.1 multiply_convert_fusion.1
  82.6 0.2 convolution_multiply_fusion.4
  82.8 0.3 fusion.30
  83.1 3.7 %collective-permute-done.3 = bf16[1024,384]{1,0:T(8,128)(2,1)S(1)} collective-permute-done((bf16[1024,384]{1,0:T(8,128)(2,1)S(1)}, bf16[1024,384]{1,0:T(8,128)(2,1)S(1)}, u32[]{:S(2)}, u32[]{:S(2)}) %collective-permute-start.3) | collective-permute-done | bytes 786464 | tf_op jit(solution)/shard_map/ppermute | solution.py:10
  86.7 1.5 multiply_reduce_fusion
  88.2 0.3 fusion.10
  88.5 1.0 multiply_reduce_fusion.5
  89.5 1.0 multiply_reduce_fusion.4
  90.5 0.3 fusion.27
  90.7 1.2 multiply_reduce_fusion.1
  91.9 0.3 fusion.17
  92.2 0.4 multiply_reduce_fusion.2
  92.6 3.8 %convolution_bitcast_fusion = f32[4096,384]{0,1:T(8,128)} fusion(bf16[128,4096]{1,0:T(8,128)(2,1)S(1)} %copy-done, f32[128,384]{1,0:T(8,128)S(1)} %get-tuple-element.35, f32[128,384]{1,0:T(8,128)S(1)} %get-tuple-element.30, f32[128]{0:T(128)S(1)} %get-tuple-element.34, f32[128]{0:T(128)S(1)} %add_rsqrt_fusion.1), kind=kOutput, calls=%fused_computation | convolution fusion | flops 402898944 | bytes 7734272 | tf_op jit(solution)/shard_map/dot_general | solution.py:92
  96.4 0.0 reduce-scatter.2.cloned.1.call-update
  102.9 35.8 %all-reduce = (f32[1]{0:T(128)}, f32[1]{0:T(128)}) all-reduce(f32[1]{0:T(128)} %bitcast.6, f32[1]{0:T(128)} %bitcast.5), channel_id=1, replica_groups=mesh['group'=2,'dp'=16] {'dp'}, use_global_device_ids=true, to_apply=%region_20.21 | all-reduce | flops 2 | bytes 16 | tf_op jit(solution)/shard_map/psum | solution.py:99
  138.7 1.9 pad_maximum_fusion
  140.6 0.5 negate_subtract_fusion
  141.1 42.0 %reduce-scatter.2.cloned.1.call-done = f32[256,384]{0,1:T(8,128)} async-done(((f32[4096,384]{0,1:T(8,128)}), f32[256,384]{0,1:T(8,128)}) %reduce-scatter.2.cloned.1.call-update) | async-done | bytes 393232 | tf_op jit(solution)/shard_map/reduce_scatter | solution.py:91
  183.1 1.9 copy.9
  (7 shorter events, 0.1 us)
Async XLA Ops:
  7.2 72.6 %copy-start = (bf16[128,4096]{1,0:T(8,128)(2,1)S(1)}, bf16[128,4096]{1,0:T(8,128)(2,1)}, u32[]{:S(2)}) copy-start(bf16[128,4096]{1,0:T(8,128)(2,1)} %param.6) | copy-start | bytes 3145732
  7.2 72.6 %all-gather.2.cloned.1.call-start = ((), (), s32[]{:S(2)}) async-start(), calls=%async_computation.1 | async-start | bytes 3342336 | tf_op jit(solution)/shard_map/all_gather | solution.py:18
  7.9 175.2 %reduce-scatter.2.cloned.1.call-start = ((), (), s32[]{:S(2)}) async-start(), calls=%async_computation.2 | async-start | bytes 6684672 | tf_op jit(solution)/shard_map/reduce_scatter | solution.py:91
  10.0 1.9 collective-permute-start
  11.9 8.1 %collective-permute-start.1 = (bf16[256,384]{1,0:T(8,128)(2,1)S(1)}, bf16[256,384]{1,0:T(8,128)(2,1)S(1)}, u32[]{:S(2)}, u32[]{:S(2)}) collective-permute-start(bf16[256,384]{1,0:T(8,128)(2,1)S(1)} %maximum_select_fusion.2), channel_id=1, source_target_pairs={{0,2},{1,3},{2,0},{3,1},{4,6},{5,7},{6,4},{7,5},{8,10},{9,11},{10,... | collective-permute-start | bytes 589832 | tf_op jit(solution)/shard_map/ppermute | solution.py:10
  20.2 17.2 %collective-permute-start.2 = (bf16[512,384]{1,0:T(8,128)(2,1)S(1)}, bf16[512,384]{1,0:T(8,128)(2,1)S(1)}, u32[]{:S(2)}, u32[]{:S(2)}) collective-permute-start(bf16[512,384]{1,0:T(8,128)(2,1)S(1)} %maximum_select_fusion.1), channel_id=1, source_target_pairs={{0,4},{1,5},{2,6},{3,7},{4,0},{5,1},{6,2},{7,3},{8,12},{9,13},{10,... | collective-permute-start | bytes 1179656 | tf_op jit(solution)/shard_map/ppermute | solution.py:10
  37.7 49.0 %collective-permute-start.3 = (bf16[1024,384]{1,0:T(8,128)(2,1)S(1)}, bf16[1024,384]{1,0:T(8,128)(2,1)S(1)}, u32[]{:S(2)}, u32[]{:S(2)}) collective-permute-start(bf16[1024,384]{1,0:T(8,128)(2,1)S(1)} %maximum_select_fusion), channel_id=1, source_target_pairs={{0,8},{1,9},{2,10},{3,11},{4,12},{5,13},{6,14},{7,15},{8,0},{9,1},... | collective-permute-start | bytes 2359304 | tf_op jit(solution)/shard_map/ppermute | solution.py:10
Sparse Core Ops, SparseCore 0:
  10.3 69.4 all-gather.1
  96.6 86.4 reduce-scatter.1
where the time goes:
time: 192 us
  waiting for transfers between devices  106 us (55%)
  blocking collectives  35.8 us (19%)
  between operations  22 us (11%)
  matrix products  12.8 us (7%)
  starting transfers between devices  7.85 us (4%)
  other arithmetic  4.99 us (3%)
  local copies, waits for them, and re-layouts  2.67 us (1%)
    reduce_scatter x1, waiting for transfers between devices, shards(): lax.psum_scatter(lax.dot_general(clips_feat, grad_proj, (((0,), (0,)), ((...  42 us
    all_gather x1, waiting for transfers between devices, shards(): full_weight = lax.all_gather(weight, 'dp', axis=0, tiled=True)  39.4 us
    psum x1, blocking collectives, shards(): summed = lax.psum((dscale, dbias), 'dp')  35.8 us
    ppermute x4, waiting for transfers between devices, swapped(): lax.ppermute(x, axis, [(i, i ^ 1 << apart) for i in range(lax.axis_size(a...  23.6 us
    ppermute x4, starting transfers between devices, swapped(): lax.ppermute(x, axis, [(i, i ^ 1 << apart) for i in range(lax.axis_size(a...  7.77 us
    dot_general x5, matrix products, one_tile(): lax.dot_general(clip_unit, block, (((1,), (1,)), ((), ())), preferred_ele...  4.8 us
  transfers between devices with their start and end apart: 6, of which 5 were waited for; matrix products, arithmetic and copies ran while one was open for 5% of the time, Pallas kernels for 0%

commit v1 on v0

--- a/solution.py
+++ b/solution.py
@@ -4,6 +4,17 @@
 from jax.sharding import PartitionSpec as P
 
 column_block = 2048
+
+
+def around_the_ring(block, name, dim):
+    size = lax.axis_size(name)
+    right = [(i, (i + 1) % size) for i in range(size)]
+    parts = [block]
+    for stride in range(1, size):
+        parts = [lax.ppermute(parts[0], name, right), *parts]
+    out = jnp.concatenate(parts, axis=dim)
+    places = (lax.axis_index(name) + 1) * parts[-1].shape[dim]
+    return jnp.roll(out, places, axis=dim)
 
 
 def swapped(x, axis, apart):
@@ -15,7 +26,7 @@
     embed_width = weight.shape[1]
     devices = lax.axis_size("dp")
     position = lax.axis_index("dp")
-    full_weight = lax.all_gather(weight, "dp", axis=0, tiled=True)
+    full_weight = around_the_ring(weight, "dp", 0)
     proj = jnp.dot(clips_feat, full_weight, preferred_element_type=jnp.float32)
     inverse = lax.rsqrt(jnp.sum(proj * proj, axis=1, keepdims=True) + 1e-06)
     unit32 = proj * inverse

time: 192 us -> 257 us (1.34)
  waiting for transfers between devices: 106 us -> 172 us
  starting transfers between devices: 7.85 us -> 0.86 us
  blocking collectives: 35.8 us -> 38.7 us
    ppermute x0 -> x15, waiting for transfers between devices: none -> 114 us  [around_the_ring(): parts = [lax.ppermute(parts[0], name, right), *parts]]
    all_gather x1 -> x0, waiting for transfers between devices: 39.4 us -> none  [shards(): full_weight = lax.all_gather(weight, 'dp', axis=0, tiled=True)]
    ppermute x4, waiting for transfers between devices: 23.6 us -> 15.6 us  [swapped(): lax.ppermute(x, axis, [(i, i ^ 1 << apart) for i in range(lax.axis_size(a...]
    ppermute x4, starting transfers between devices: 7.77 us -> 0.29 us  [swapped(): lax.ppermute(x, axis, [(i, i ^ 1 << apart) for i in range(lax.axis_size(a...]
    psum x1, blocking collectives: 35.8 us -> 38.7 us  [shards(): summed = lax.psum((dscale, dbias), 'dp')]
  transfers between devices with their start and end apart: 6 -> 20, of which waited for: 5 -> 17; matrix products, arithmetic and copies ran while one was open for 5% -> 4% of each run, Pallas kernels for 0% -> 0%
where the time goes in v1:
time: 257 us
  waiting for transfers between devices  172 us (67%)
  blocking collectives  38.7 us (15%)
  between operations  22.3 us (9%)
  matrix products  13 us (5%)
  other arithmetic  5.89 us (2%)
  local copies, waits for them, and re-layouts  3.73 us (1%)
    ppermute x15, waiting for transfers between devices, around_the_ring(): parts = [lax.ppermute(parts[0], name, right), *parts]  114 us
    reduce_scatter x1, waiting for transfers between devices, shards(): lax.psum_scatter(lax.dot_general(clips_feat, grad_proj, (((0,), (0,)), ((...  42.4 us
    psum x1, blocking collectives, shards(): summed = lax.psum((dscale, dbias), 'dp')  38.7 us
    ppermute x4, waiting for transfers between devices, swapped(): lax.ppermute(x, axis, [(i, i ^ 1 << apart) for i in range(lax.axis_size(a...  15.6 us
    dot_general x5, matrix products, one_tile(): lax.dot_general(clip_unit, block, (((1,), (1,)), ((), ())), preferred_ele...  5.67 us
  transfers between devices with their start and end apart: 20, of which 17 were waited for; matrix products, arithmetic and copies ran while one was open for 4% of the time, Pallas kernels for 0%

profile of v1, /device:TPU:0, one launch (start us, length us, event | category | flops | bytes accessed | tf_op | source)
XLA Modules:
  0.0 256.7 jit_solution(2316912348758481467)
XLA Ops:
  7.2 0.0 copy-start
  7.2 0.0 reduce-scatter.2.cloned.1.call-start
  7.2 0.5 collective-permute-start
  7.7 8.5 %collective-permute-done = bf16[256,384]{1,0:T(8,128)(2,1)S(1)} collective-permute-done((bf16[256,384]{1,0:T(8,128)(2,1)}, bf16[256,384]{1,0:T(8,128)(2,1)S(1)}, u32[]{:S(2)}, u32[]{:S(2)}) %collective-permute-start) | collective-permute-done | bytes 196640 | tf_op jit(solution)/shard_map/ppermute | solution.py:14
  16.3 0.0 collective-permute-start.1
  16.3 7.8 %collective-permute-done.1 = bf16[256,384]{1,0:T(8,128)(2,1)S(1)} collective-permute-done((bf16[256,384]{1,0:T(8,128)(2,1)S(1)}, bf16[256,384]{1,0:T(8,128)(2,1)S(1)}, u32[]{:S(2)}, u32[]{:S(2)}) %collective-permute-start.1) | collective-permute-done | bytes 196640 | tf_op jit(solution)/shard_map/ppermute | solution.py:14
  24.1 0.0 collective-permute-start.2
  24.1 7.8 %collective-permute-done.2 = bf16[256,384]{1,0:T(8,128)(2,1)S(1)} collective-permute-done((bf16[256,384]{1,0:T(8,128)(2,1)S(1)}, bf16[256,384]{1,0:T(8,128)(2,1)S(1)}, u32[]{:S(2)}, u32[]{:S(2)}) %collective-permute-start.2) | collective-permute-done | bytes 196640 | tf_op jit(solution)/shard_map/ppermute | solution.py:14
  31.9 0.0 collective-permute-start.3
  31.9 7.8 %collective-permute-done.3 = bf16[256,384]{1,0:T(8,128)(2,1)S(1)} collective-permute-done((bf16[256,384]{1,0:T(8,128)(2,1)S(1)}, bf16[256,384]{1,0:T(8,128)(2,1)S(1)}, u32[]{:S(2)}, u32[]{:S(2)}) %collective-permute-start.3) | collective-permute-done | bytes 196640 | tf_op jit(solution)/shard_map/ppermute | solution.py:14
  39.6 0.0 collective-permute-start.4
  39.6 7.8 %collective-permute-done.4 = bf16[256,384]{1,0:T(8,128)(2,1)S(1)} collective-permute-done((bf16[256,384]{1,0:T(8,128)(2,1)S(1)}, bf16[256,384]{1,0:T(8,128)(2,1)S(1)}, u32[]{:S(2)}, u32[]{:S(2)}) %collective-permute-start.4) | collective-permute-done | bytes 196640 | tf_op jit(solution)/shard_map/ppermute | solution.py:14
  47.4 0.0 collective-permute-start.5
  47.4 7.8 %collective-permute-done.5 = bf16[256,384]{1,0:T(8,128)(2,1)S(1)} collective-permute-done((bf16[256,384]{1,0:T(8,128)(2,1)S(1)}, bf16[256,384]{1,0:T(8,128)(2,1)S(1)}, u32[]{:S(2)}, u32[]{:S(2)}) %collective-permute-start.5) | collective-permute-done | bytes 196640 | tf_op jit(solution)/shard_map/ppermute | solution.py:14
  55.2 0.0 collective-permute-start.6
  55.2 7.8 %collective-permute-done.6 = bf16[256,384]{1,0:T(8,128)(2,1)S(1)} collective-permute-done((bf16[256,384]{1,0:T(8,128)(2,1)S(1)}, bf16[256,384]{1,0:T(8,128)(2,1)S(1)}, u32[]{:S(2)}, u32[]{:S(2)}) %collective-permute-start.6) | collective-permute-done | bytes 196640 | tf_op jit(solution)/shard_map/ppermute | solution.py:14
  63.0 0.0 collective-permute-start.7
  63.0 1.0 fusion.14
  64.0 6.8 %collective-permute-done.7 = bf16[256,384]{1,0:T(8,128)(2,1)S(1)} collective-permute-done((bf16[256,384]{1,0:T(8,128)(2,1)S(1)}, bf16[256,384]{1,0:T(8,128)(2,1)S(1)}, u32[]{:S(2)}, u32[]{:S(2)}) %collective-permute-start.7) | collective-permute-done | bytes 196640 | tf_op jit(solution)/shard_map/ppermute | solution.py:14
  70.8 0.0 collective-permute-start.8
  70.8 7.8 %collective-permute-done.8 = bf16[256,384]{1,0:T(8,128)(2,1)S(1)} collective-permute-done((bf16[256,384]{1,0:T(8,128)(2,1)S(1)}, bf16[256,384]{1,0:T(8,128)(2,1)S(1)}, u32[]{:S(2)}, u32[]{:S(2)}) %collective-permute-start.8) | collective-permute-done | bytes 196640 | tf_op jit(solution)/shard_map/ppermute | solution.py:14
  78.6 0.0 collective-permute-start.9
  78.6 1.0 fusion.15
  79.6 0.1 collective-permute-start.15
  79.7 6.8 %collective-permute-done.9 = bf16[256,384]{1,0:T(8,128)(2,1)S(1)} collective-permute-done((bf16[256,384]{1,0:T(8,128)(2,1)S(1)}, bf16[256,384]{1,0:T(8,128)(2,1)S(1)}, u32[]{:S(2)}, u32[]{:S(2)}) %collective-permute-start.9) | collective-permute-done | bytes 196640 | tf_op jit(solution)/shard_map/ppermute | solution.py:14
  86.5 0.0 collective-permute-start.10
  87.9 0.0 collective-permute-done.15
  87.9 1.0 maximum_select_fusion.2
  89.0 0.1 collective-permute-start.16
  89.0 5.4 %collective-permute-done.10 = bf16[256,384]{1,0:T(8,128)(2,1)S(1)} collective-permute-done((bf16[256,384]{1,0:T(8,128)(2,1)S(1)}, bf16[256,384]{1,0:T(8,128)(2,1)S(1)}, u32[]{:S(2)}, u32[]{:S(2)}) %collective-permute-start.10) | collective-permute-done | bytes 196640 | tf_op jit(solution)/shard_map/ppermute | solution.py:14
  94.4 0.0 collective-permute-start.11
  94.4 7.9 %collective-permute-done.11 = bf16[256,384]{1,0:T(8,128)(2,1)S(1)} collective-permute-done((bf16[256,384]{1,0:T(8,128)(2,1)S(1)}, bf16[256,384]{1,0:T(8,128)(2,1)S(1)}, u32[]{:S(2)}, u32[]{:S(2)}) %collective-permute-start.11) | collective-permute-done | bytes 196640 | tf_op jit(solution)/shard_map/ppermute | solution.py:14
  102.3 0.0 collective-permute-start.12
  102.3 0.0 collective-permute-done.16
  102.3 0.1 maximum_select_fusion.1
  102.5 0.1 collective-permute-start.17
  102.5 7.5 %collective-permute-done.12 = bf16[256,384]{1,0:T(8,128)(2,1)S(1)} collective-permute-done((bf16[256,384]{1,0:T(8,128)(2,1)S(1)}, bf16[256,384]{1,0:T(8,128)(2,1)S(1)}, u32[]{:S(2)}, u32[]{:S(2)}) %collective-permute-start.12) | collective-permute-done | bytes 196640 | tf_op jit(solution)/shard_map/ppermute | solution.py:14
  110.1 0.0 collective-permute-start.13
  110.1 0.8 slice_bitcast_fusion.1
  110.9 7.1 %collective-permute-done.13 = bf16[256,384]{1,0:T(8,128)(2,1)S(1)} collective-permute-done((bf16[256,384]{1,0:T(8,128)(2,1)S(1)}, bf16[256,384]{1,0:T(8,128)(2,1)S(1)}, u32[]{:S(2)}, u32[]{:S(2)}) %collective-permute-start.13) | collective-permute-done | bytes 196640 | tf_op jit(solution)/shard_map/ppermute | solution.py:14
  118.0 0.0 collective-permute-start.14
  118.0 0.0 collective-permute-done.17
  118.0 0.3 maximum_select_fusion
  118.3 0.1 collective-permute-start.18
  118.4 9.6 %collective-permute-done.14 = bf16[256,384]{1,0:T(8,128)(2,1)S(1)} collective-permute-done((bf16[256,384]{1,0:T(8,128)(2,1)S(1)}, bf16[256,384]{1,0:T(8,128)(2,1)S(1)}, u32[]{:S(2)}, u32[]{:S(2)}) %collective-permute-start.14) | collective-permute-done | bytes 196640 | tf_op jit(solution)/shard_map/ppermute | solution.py:14
  129.3 1.1 multiply_reduce_fusion.2
  130.4 0.2 convolution_multiply_fusion.4
  130.6 0.3 fusion.38
  130.9 15.6 %collective-permute-done.18 = bf16[1024,384]{1,0:T(8,128)(2,1)S(1)} collective-permute-done((bf16[1024,384]{1,0:T(8,128)(2,1)S(1)}, bf16[1024,384]{1,0:T(8,128)(2,1)S(1)}, u32[]{:S(2)}, u32[]{:S(2)}) %collective-permute-start.18) | collective-permute-done | bytes 786464 | tf_op jit(solution)/shard_map/ppermute | solution.py:21
  146.5 1.5 multiply_reduce_fusion
  148.0 0.4 fusion.12
  148.4 1.8 multiply_reduce_fusion.4
  150.2 1.0 multiply_reduce_fusion.3
  151.2 1.2 multiply_reduce_fusion.1
  152.4 0.4 fusion.23
  152.9 0.3 fusion.35
  153.2 1.2 fusion.16
  154.4 3.6 %convolution_bitcast_fusion = f32[4096,384]{0,1:T(8,128)} fusion(bf16[128,4096]{1,0:T(8,128)(2,1)S(1)} %copy-done, f32[128,384]{0,1:T(8,128)S(1)} %get-tuple-element.35, f32[384,128]{1,0:T(8,128)S(1)} %get-tuple-element.30, f32[128]{0:T(128)S(1)} %get-tuple-element.34, f32[128]{0:T(128)S(1)} %add_rsqrt_fusion.1), kind=kOutput, calls=%fused_computation | convolution fusion | flops 402898944 | bytes 7734272 | tf_op jit(solution)/shard_map/dot_general | solution.py:103
  158.0 0.0 reduce-scatter.2.cloned.1.call-update
  164.5 38.7 %all-reduce = (f32[1]{0:T(128)}, f32[1]{0:T(128)}) all-reduce(f32[1]{0:T(128)} %bitcast.7, f32[1]{0:T(128)} %bitcast.6), channel_id=1, replica_groups=mesh['group'=2,'dp'=16] {'dp'}, use_global_device_ids=true, to_apply=%region_20.21 | all-reduce | flops 2 | bytes 16 | tf_op jit(solution)/shard_map/psum | solution.py:110
  203.2 1.9 pad_maximum_fusion
  205.0 0.5 negate_subtract_fusion
  205.6 42.4 %reduce-scatter.2.cloned.1.call-done = f32[256,384]{0,1:T(8,128)} async-done(((f32[4096,384]{0,1:T(8,128)}), f32[256,384]{0,1:T(8,128)}) %reduce-scatter.2.cloned.1.call-update) | async-done | bytes 393232 | tf_op jit(solution)/shard_map/reduce_scatter | solution.py:102
  248.0 1.9 copy.14
  (42 shorter events, 1.1 us)
Async XLA Ops:
  7.2 122.1 %copy-start = (bf16[128,4096]{1,0:T(8,128)(2,1)S(1)}, bf16[128,4096]{1,0:T(8,128)(2,1)}, u32[]{:S(2)}) copy-start(bf16[128,4096]{1,0:T(8,128)(2,1)} %param.6) | copy-start | bytes 3145732
  7.2 121.4 %copy-start.1 = (bf16[256,384]{1,0:T(8,128)(2,1)S(1)}, bf16[256,384]{1,0:T(8,128)(2,1)}, u32[]{:S(2)}) copy-start(bf16[256,384]{1,0:T(8,128)(2,1)} %param.7) | copy-start | bytes 589828
  7.2 240.8 %reduce-scatter.2.cloned.1.call-start = ((), (), s32[]{:S(2)}) async-start(), calls=%async_computation.1 | async-start | bytes 6684672 | tf_op jit(solution)/shard_map/reduce_scatter | solution.py:102
  7.2 9.0 %collective-permute-start = (bf16[256,384]{1,0:T(8,128)(2,1)}, bf16[256,384]{1,0:T(8,128)(2,1)S(1)}, u32[]{:S(2)}, u32[]{:S(2)}) collective-permute-start(bf16[256,384]{1,0:T(8,128)(2,1)} %param.7), channel_id=1, source_target_pairs={{0,1},{1,2},{2,3},{3,4},{4,5},{5,6},{6,7},{7,8},{8,9},{9,10},{10,1... | collective-permute-start | bytes 589832 | tf_op jit(solution)/shard_map/ppermute | solution.py:14
  16.3 7.8 %collective-permute-start.1 = (bf16[256,384]{1,0:T(8,128)(2,1)S(1)}, bf16[256,384]{1,0:T(8,128)(2,1)S(1)}, u32[]{:S(2)}, u32[]{:S(2)}) collective-permute-start(bf16[256,384]{1,0:T(8,128)(2,1)S(1)} %collective-permute-done), channel_id=1, source_target_pairs={{0,1},{1,2},{2,3},{3,4},{4,5},{5,6},{6,7},{7,8},{8,9},{9,10},{10,1... | collective-permute-start | bytes 589832 | tf_op jit(solution)/shard_map/ppermute | solution.py:14
  24.1 7.8 %collective-permute-start.2 = (bf16[256,384]{1,0:T(8,128)(2,1)S(1)}, bf16[256,384]{1,0:T(8,128)(2,1)S(1)}, u32[]{:S(2)}, u32[]{:S(2)}) collective-permute-start(bf16[256,384]{1,0:T(8,128)(2,1)S(1)} %collective-permute-done.1), channel_id=1, source_target_pairs={{0,1},{1,2},{2,3},{3,4},{4,5},{5,6},{6,7},{7,8},{8,9},{9,10},{10,1... | collective-permute-start | bytes 589832 | tf_op jit(solution)/shard_map/ppermute | solution.py:14
  31.9 7.8 %collective-permute-start.3 = (bf16[256,384]{1,0:T(8,128)(2,1)S(1)}, bf16[256,384]{1,0:T(8,128)(2,1)S(1)}, u32[]{:S(2)}, u32[]{:S(2)}) collective-permute-start(bf16[256,384]{1,0:T(8,128)(2,1)S(1)} %collective-permute-done.2), channel_id=1, source_target_pairs={{0,1},{1,2},{2,3},{3,4},{4,5},{5,6},{6,7},{7,8},{8,9},{9,10},{10,1... | collective-permute-start | bytes 589832 | tf_op jit(solution)/shard_map/ppermute | solution.py:14
  39.6 7.8 %collective-permute-start.4 = (bf16[256,384]{1,0:T(8,128)(2,1)S(1)}, bf16[256,384]{1,0:T(8,128)(2,1)S(1)}, u32[]{:S(2)}, u32[]{:S(2)}) collective-permute-start(bf16[256,384]{1,0:T(8,128)(2,1)S(1)} %collective-permute-done.3), channel_id=1, source_target_pairs={{0,1},{1,2},{2,3},{3,4},{4,5},{5,6},{6,7},{7,8},{8,9},{9,10},{10,1... | collective-permute-start | bytes 589832 | tf_op jit(solution)/shard_map/ppermute | solution.py:14
  47.4 7.8 %collective-permute-start.5 = (bf16[256,384]{1,0:T(8,128)(2,1)S(1)}, bf16[256,384]{1,0:T(8,128)(2,1)S(1)}, u32[]{:S(2)}, u32[]{:S(2)}) collective-permute-start(bf16[256,384]{1,0:T(8,128)(2,1)S(1)} %collective-permute-done.4), channel_id=1, source_target_pairs={{0,1},{1,2},{2,3},{3,4},{4,5},{5,6},{6,7},{7,8},{8,9},{9,10},{10,1... | collective-permute-start | bytes 589832 | tf_op jit(solution)/shard_map/ppermute | solution.py:14
  55.2 7.8 %collective-permute-start.6 = (bf16[256,384]{1,0:T(8,128)(2,1)S(1)}, bf16[256,384]{1,0:T(8,128)(2,1)S(1)}, u32[]{:S(2)}, u32[]{:S(2)}) collective-permute-start(bf16[256,384]{1,0:T(8,128)(2,1)S(1)} %collective-permute-done.5), channel_id=1, source_target_pairs={{0,1},{1,2},{2,3},{3,4},{4,5},{5,6},{6,7},{7,8},{8,9},{9,10},{10,1... | collective-permute-start | bytes 589832 | tf_op jit(solution)/shard_map/ppermute | solution.py:14
  63.0 7.8 %collective-permute-start.7 = (bf16[256,384]{1,0:T(8,128)(2,1)S(1)}, bf16[256,384]{1,0:T(8,128)(2,1)S(1)}, u32[]{:S(2)}, u32[]{:S(2)}) collective-permute-start(bf16[256,384]{1,0:T(8,128)(2,1)S(1)} %collective-permute-done.6), channel_id=1, source_target_pairs={{0,1},{1,2},{2,3},{3,4},{4,5},{5,6},{6,7},{7,8},{8,9},{9,10},{10,1... | collective-permute-start | bytes 589832 | tf_op jit(solution)/shard_map/ppermute | solution.py:14
  70.8 7.8 %collective-permute-start.8 = (bf16[256,384]{1,0:T(8,128)(2,1)S(1)}, bf16[256,384]{1,0:T(8,128)(2,1)S(1)}, u32[]{:S(2)}, u32[]{:S(2)}) collective-permute-start(bf16[256,384]{1,0:T(8,128)(2,1)S(1)} %collective-permute-done.7), channel_id=1, source_target_pairs={{0,1},{1,2},{2,3},{3,4},{4,5},{5,6},{6,7},{7,8},{8,9},{9,10},{10,1... | collective-permute-start | bytes 589832 | tf_op jit(solution)/shard_map/ppermute | solution.py:14
  78.6 7.9 %collective-permute-start.9 = (bf16[256,384]{1,0:T(8,128)(2,1)S(1)}, bf16[256,384]{1,0:T(8,128)(2,1)S(1)}, u32[]{:S(2)}, u32[]{:S(2)}) collective-permute-start(bf16[256,384]{1,0:T(8,128)(2,1)S(1)} %collective-permute-done.8), channel_id=1, source_target_pairs={{0,1},{1,2},{2,3},{3,4},{4,5},{5,6},{6,7},{7,8},{8,9},{9,10},{10,1... | collective-permute-start | bytes 589832 | tf_op jit(solution)/shard_map/ppermute | solution.py:14
  79.6 8.3 %collective-permute-start.15 = (bf16[128,384]{1,0:T(8,128)(2,1)S(1)}, bf16[128,384]{1,0:T(8,128)(2,1)}, u32[]{:S(2)}, u32[]{:S(2)}) collective-permute-start(bf16[128,384]{1,0:T(8,128)(2,1)S(1)} %fusion.15), channel_id=1, source_target_pairs={{0,1},{1,0},{2,3},{3,2},{4,5},{5,4},{6,7},{7,6},{8,9},{9,8},{10,11... | collective-permute-start | bytes 294920 | tf_op jit(solution)/shard_map/ppermute | solution.py:21
  86.5 7.9 %collective-permute-start.10 = (bf16[256,384]{1,0:T(8,128)(2,1)S(1)}, bf16[256,384]{1,0:T(8,128)(2,1)S(1)}, u32[]{:S(2)}, u32[]{:S(2)}) collective-permute-start(bf16[256,384]{1,0:T(8,128)(2,1)S(1)} %collective-permute-done.9), channel_id=1, source_target_pairs={{0,1},{1,2},{2,3},{3,4},{4,5},{5,6},{6,7},{7,8},{8,9},{9,10},{10,1... | collective-permute-start | bytes 589832 | tf_op jit(solution)/shard_map/ppermute | solution.py:14
  89.0 13.4 %collective-permute-start.16 = (bf16[256,384]{1,0:T(8,128)(2,1)S(1)}, bf16[256,384]{1,0:T(8,128)(2,1)S(1)}, u32[]{:S(2)}, u32[]{:S(2)}) collective-permute-start(bf16[256,384]{1,0:T(8,128)(2,1)S(1)} %maximum_select_fusion.2), channel_id=1, source_target_pairs={{0,2},{1,3},{2,0},{3,1},{4,6},{5,7},{6,4},{7,5},{8,10},{9,11},{10,... | collective-permute-start | bytes 589832 | tf_op jit(solution)/shard_map/ppermute | solution.py:21
  94.4 7.9 %collective-permute-start.11 = (bf16[256,384]{1,0:T(8,128)(2,1)S(1)}, bf16[256,384]{1,0:T(8,128)(2,1)S(1)}, u32[]{:S(2)}, u32[]{:S(2)}) collective-permute-start(bf16[256,384]{1,0:T(8,128)(2,1)S(1)} %collective-permute-done.10), channel_id=1, source_target_pairs={{0,1},{1,2},{2,3},{3,4},{4,5},{5,6},{6,7},{7,8},{8,9},{9,10},{10,1... | collective-permute-start | bytes 589832 | tf_op jit(solution)/shard_map/ppermute | solution.py:14
  102.3 7.8 %collective-permute-start.12 = (bf16[256,384]{1,0:T(8,128)(2,1)S(1)}, bf16[256,384]{1,0:T(8,128)(2,1)S(1)}, u32[]{:S(2)}, u32[]{:S(2)}) collective-permute-start(bf16[256,384]{1,0:T(8,128)(2,1)S(1)} %collective-permute-done.11), channel_id=1, source_target_pairs={{0,1},{1,2},{2,3},{3,4},{4,5},{5,6},{6,7},{7,8},{8,9},{9,10},{10,1... | collective-permute-start | bytes 589832 | tf_op jit(solution)/shard_map/ppermute | solution.py:14
  102.5 15.5 %collective-permute-start.17 = (bf16[512,384]{1,0:T(8,128)(2,1)S(1)}, bf16[512,384]{1,0:T(8,128)(2,1)S(1)}, u32[]{:S(2)}, u32[]{:S(2)}) collective-permute-start(bf16[512,384]{1,0:T(8,128)(2,1)S(1)} %maximum_select_fusion.1), channel_id=1, source_target_pairs={{0,4},{1,5},{2,6},{3,7},{4,0},{5,1},{6,2},{7,3},{8,12},{9,13},{10,... | collective-permute-start | bytes 1179656 | tf_op jit(solution)/shard_map/ppermute | solution.py:21
  110.1 7.9 %collective-permute-start.13 = (bf16[256,384]{1,0:T(8,128)(2,1)S(1)}, bf16[256,384]{1,0:T(8,128)(2,1)S(1)}, u32[]{:S(2)}, u32[]{:S(2)}) collective-permute-start(bf16[256,384]{1,0:T(8,128)(2,1)S(1)} %collective-permute-done.12), channel_id=1, source_target_pairs={{0,1},{1,2},{2,3},{3,4},{4,5},{5,6},{6,7},{7,8},{8,9},{9,10},{10,1... | collective-permute-start | bytes 589832 | tf_op jit(solution)/shard_map/ppermute | solution.py:14
  118.0 10.0 %collective-permute-start.14 = (bf16[256,384]{1,0:T(8,128)(2,1)S(1)}, bf16[256,384]{1,0:T(8,128)(2,1)S(1)}, u32[]{:S(2)}, u32[]{:S(2)}) collective-permute-start(bf16[256,384]{1,0:T(8,128)(2,1)S(1)} %collective-permute-done.13), channel_id=1, source_target_pairs={{0,1},{1,2},{2,3},{3,4},{4,5},{5,6},{6,7},{7,8},{8,9},{9,10},{10,1... | collective-permute-start | bytes 589832 | tf_op jit(solution)/shard_map/ppermute | solution.py:14
  118.3 28.2 %collective-permute-start.18 = (bf16[1024,384]{1,0:T(8,128)(2,1)S(1)}, bf16[1024,384]{1,0:T(8,128)(2,1)S(1)}, u32[]{:S(2)}, u32[]{:S(2)}) collective-permute-start(bf16[1024,384]{1,0:T(8,128)(2,1)S(1)} %maximum_select_fusion), channel_id=1, source_target_pairs={{0,8},{1,9},{2,10},{3,11},{4,12},{5,13},{6,14},{7,15},{8,0},{9,1},... | collective-permute-start | bytes 2359304 | tf_op jit(solution)/shard_map/ppermute | solution.py:21
Sparse Core Ops, SparseCore 0:
  158.2 89.7 reduce-scatter.1
